TPU v7x, 512 devices: a whole 4x8x8 slice. The times are simulated.
512 devices in a mesh: row: 16 (over y, core), col: 32 (over z, x).
Axes of the slice: x: 4, y: 8, z: 8, core: 2. Of those that a mesh axis runs over, the one named last changes fastest.
Arguments:
- old_vectors: float32 [8192, 4096], P('row', 'col'), may hold values from -6 to 6, as said below
- pole_values: float32 [8192], replicated, may hold values from 0 to 8192, as said below
- live_mask: int32 [8192], replicated, may hold values from 0 to 1, as said below
- position: int32 [8192], replicated, may hold values from 0 to 8191, as said below
- rank_weight: float32 [1], replicated, may hold values from 0.5 to 2
Outputs:
- new_vectors: float32 [8192, 8192], P('row', 'col')
Inputs may be any that keep to these rules, and one draw needn't show every extreme that they name: `pole_values`: strictly increasing; consecutive values differ by 0.2 or more. `old_vectors`: the entries of rows 4095 and 4096 have magnitude 0.5 to 1.5. Each merged position appears exactly once. In every aligned group of 16 consecutive columns s of the halves' eigenvectors (s = h * 4096 + m), exactly 12 have live_mask[position[s]] = 1.
All inputs are finite; a program needn't handle non-finite values.
Results may differ from a plain program's by a relative error of at most 0.0003.
Values sent between devices are 32-bit elements; how exact they have to be, the bound alone decides.
A program may use at most 64 MiB of HBM per device.

v0:
```python
import jax
import jax.numpy as jnp
from jax import lax
from jax.sharding import PartitionSpec as P

BISECT = 40


def bracket_lengths(pole_values, live_mask, squares, rank_value):
    order_size = pole_values.shape[0]
    positions = jnp.arange(order_size, dtype=jnp.int32)
    marked = jnp.where(live_mask > 0, positions, order_size)
    shifted = jnp.concatenate([marked[1:], jnp.full((1,), order_size, jnp.int32)])
    following = lax.cummin(shifted, axis=0, reverse=True)
    weight_sum = rank_value * jnp.sum(squares)
    next_gap = pole_values[jnp.minimum(following, order_size - 1)] - pole_values
    return jnp.where(following < order_size, next_gap, weight_sum)


def bisect_roots(pole_here, bracket_len, pole_values, squares, live_mask, rank_value):
    pole_diff = pole_values[None, :] - pole_here[:, None]
    alive_cols = (live_mask > 0)[None, :]

    def halving(interval, unused):
        low_end, high_end = interval
        middle = 0.5 * (low_end + high_end)
        offset_gap = pole_diff - middle[:, None]
        summands = jnp.where(
            alive_cols, squares[None, :] / jnp.where(alive_cols, offset_gap, 1.0), 0.0
        )
        secular = 1.0 + rank_value * jnp.sum(summands, axis=1)
        is_below = secular < 0.0
        return ((jnp.where(is_below, middle, low_end), jnp.where(is_below, high_end, middle)), None)

    interval, unused = lax.scan(
        halving, (jnp.zeros_like(bracket_len), bracket_len), None, length=BISECT
    )
    return 0.5 * (interval[0] + interval[1])


def log_terms(pole_here, offsets, live_here, own_index, pole_values, live_mask):
    order_size = pole_values.shape[0]
    pole_diff = pole_values[None, :] - pole_here[:, None]
    on_pole = own_index[:, None] == jnp.arange(order_size, dtype=jnp.int32)[None, :]
    quotient = jnp.where(
        on_pole, offsets[:, None], 1.0 - offsets[:, None] / jnp.where(on_pole, 1.0, pole_diff)
    )
    in_play = (live_here[:, None] > 0) & (live_mask[None, :] > 0)
    logs = jnp.where(in_play, jnp.log(jnp.abs(jnp.where(in_play, quotient, 1.0))), 0.0)
    return jnp.sum(logs, axis=0)


def column_norms(pole_here, offsets, live_here, pole_values, live_mask, hat_weights):
    alive_cols = (live_mask > 0)[None, :]
    offset_gap = pole_values[None, :] - pole_here[:, None] - offsets[:, None]
    summands = jnp.where(
        alive_cols, hat_weights[None, :] ** 2 / jnp.where(alive_cols, offset_gap, 1.0) ** 2, 0.0
    )
    return jnp.where(live_here > 0, jnp.sqrt(jnp.sum(summands, axis=1)), 1.0)


def cauchy_tile(
    sorted_rows,
    pole_cols,
    offset_cols,
    norm_cols,
    live_cols,
    col_index,
    pole_values,
    live_mask,
    hat_weights,
):
    row_poles = pole_values[sorted_rows]
    row_hats = hat_weights[sorted_rows]
    row_live = live_mask[sorted_rows] > 0
    col_live = (live_cols > 0)[None, :]
    both_live = row_live[:, None] & col_live
    offset_gap = row_poles[:, None] - pole_cols[None, :] - offset_cols[None, :]
    entries = row_hats[:, None] / jnp.where(both_live, offset_gap, 1.0) / norm_cols[None, :]
    identity = (sorted_rows[:, None] == col_index[None, :]).astype(jnp.float32)
    return jnp.where(col_live, jnp.where(both_live, entries, 0.0), identity)


def hat_from(log_sum, coupling, live_mask, rank_value):
    return jnp.where(
        live_mask > 0, jnp.sign(coupling) * jnp.exp(0.5 * (log_sum - jnp.log(rank_value))), 0.0
    )


def shards(old_vectors, pole_values, live_mask, position, rank_weight):
    rank_value = rank_weight[0]
    order_size = pole_values.shape[0]
    half_order = order_size // 2
    rows_here = old_vectors.shape[0]
    row_count = lax.axis_size("row")
    col_count = lax.axis_size("col")
    row_rank = lax.axis_index("row")
    col_rank = lax.axis_index("col")
    upper_owner = (half_order - 1) // rows_here
    lower_owner = half_order // rows_here
    edge_rows = jnp.stack(
        [
            jnp.where(row_rank == upper_owner, old_vectors[(half_order - 1) % rows_here], 0.0),
            jnp.where(row_rank == lower_owner, old_vectors[half_order % rows_here], 0.0),
        ]
    )
    edge_rows = lax.psum(edge_rows, "row")
    edge_rows = lax.all_gather(edge_rows, "col", axis=1, tiled=True)
    boundary = jnp.concatenate([edge_rows[0], edge_rows[1]])
    spread = jnp.zeros((order_size,), jnp.float32).at[position].set(boundary)
    coupling = jnp.where(live_mask > 0, spread, 0.0)
    squares = coupling * coupling
    bracket_len = bracket_lengths(pole_values, live_mask, squares, rank_value)
    block_cols = order_size // col_count
    per_device = block_cols // row_count
    block_first = col_rank * block_cols
    own_first = block_first + row_rank * per_device
    block_index = block_first + jnp.arange(block_cols, dtype=jnp.int32)
    own_poles = lax.dynamic_slice_in_dim(pole_values, own_first, per_device)
    own_live = lax.dynamic_slice_in_dim(live_mask, own_first, per_device)
    own_bracket = lax.dynamic_slice_in_dim(bracket_len, own_first, per_device)
    block_poles = lax.dynamic_slice_in_dim(pole_values, block_first, block_cols)
    block_live = lax.dynamic_slice_in_dim(live_mask, block_first, block_cols)
    bisected = bisect_roots(own_poles, own_bracket, pole_values, squares, live_mask, rank_value)
    own_offsets = jnp.where(own_live > 0, bisected, 0.5 * own_bracket)
    block_offsets = lax.all_gather(own_offsets, "row", axis=0, tiled=True)
    grouped = (
        block_poles.reshape(row_count, per_device),
        block_offsets.reshape(row_count, per_device),
        block_live.reshape(row_count, per_device),
        block_index.reshape(row_count, per_device),
    )

    def log_group(members):
        return log_terms(members[0], members[1], members[2], members[3], pole_values, live_mask)

    partial_logs = jnp.sum(lax.map(log_group, grouped), axis=0)
    log_sum = lax.psum(partial_logs, "col")
    hat_weights = hat_from(log_sum, coupling, live_mask, rank_value)

    def norm_group(members):
        return column_norms(members[0], members[1], members[2], pole_values, live_mask, hat_weights)

    block_norms = lax.map(norm_group, (grouped[0], grouped[1], grouped[2])).reshape(block_cols)
    half_id = row_rank * rows_here // half_order
    half_base = half_id * half_order
    panel_piece = lax.all_gather(old_vectors, "col", axis=1, tiled=True)
    sorted_rows = lax.dynamic_slice_in_dim(position, half_base, panel_piece.shape[1])
    cauchy = cauchy_tile(
        sorted_rows,
        block_poles,
        block_offsets,
        block_norms,
        block_live,
        block_index,
        pole_values,
        live_mask,
        hat_weights,
    )
    return jnp.dot(
        panel_piece, cauchy, precision=lax.Precision.HIGHEST, preferred_element_type=jnp.float32
    )


def solution(mesh):
    in_specs = (P("row", "col"), P(), P(), P(), P())
    out_specs = P("row", "col")
    return jax.shard_map(shards, mesh=mesh, in_specs=in_specs, out_specs=out_specs, check_vma=False)
```

profile of v0, /device:TPU:32, one launch (start us, length us, event | category | flops | bytes accessed | tf_op | source)
XLA Modules:
  0.0 492.8 jit_solution(11255109670068731941)
XLA Ops:
  6.5 0.7 all-gather.2.cloned.1.call-update
  7.3 0.7 broadcast_select_fusion.2
  8.0 23.6 %psum.14 = f32[2,128]{1,0:T(2,128)S(1)} all-reduce(f32[2,128]{1,0:T(2,128)S(1)} %pad_maximum_fusion.1), channel_id=1, replica_groups=mesh['row'=16,'col'=32] {'row'}, use_global_device_ids=true, to_apply=%region_0.1 | all-reduce | flops 256 | bytes 2048 | tf_op jit(solution)/shard_map/psum | solution.py:107
  31.5 49.0 %all_gather.9 = f32[2,4096]{1,0:T(2,128)S(1)} all-gather(f32[2,128]{1,0:T(2,128)S(1)} %psum.14), channel_id=1, replica_groups=mesh['row'=16,'col'=32] {'col'}, dimensions={1}, use_global_device_ids=true | all-gather | bytes 33792 | tf_op jit(solution)/shard_map/all_gather | solution.py:108
  80.6 0.8 compare_select_fusion.4
  81.4 30.5 %scatter_custom_fusion = f32[8192]{0:T(1024)S(1)} fusion(s32[8192]{0:T(1024)S(1)} %compare_select_fusion.4, f32[8192]{0:T(1024)S(1)} %pad_maximum_fusion, f32[]{:T(128)} %constant.114.clone.1), kind=kCustom, calls=%fused_computation.74 | custom fusion | bytes 32772 | tf_op jit(solution)/shard_map/scatter | solution.py:110
  111.9 1.4 fusion.44
  113.4 2.3 reduce-window.9
  115.7 0.6 reduce-window.12
  116.8 0.8 broadcast_compare_fusion.4
  117.5 0.8 dynamic_slice.52
  118.3 45.5 %gather_fusion.1 = f32[8192]{0:T(1024)S(1)} fusion(f32[8192]{0:T(1024)S(1)} %copy-done, s32[8192]{0:T(1024)S(1)} %broadcast_clamp_fusion), kind=kCustom, calls=%fused_computation.1 | custom fusion | bytes 98304 | tf_op jit(solution)/shard_map/gather | solution.py:16
  165.1 46.3 %while.37 = (s32[]{:T(128)}, f32[16]{0:T(128)S(1)}, f32[16]{0:T(128)S(1)}, f32[]{:T(128)}, pred[1,8192]{1,0:T(4,128)(4,1)S(1)}, /*index=5*/f32[8192]{0:T(1024)S(...) while((s32[]{:T(128)}, f32[16]{0:T(128)S(1)}, ...), condition=%wide.region_7.8_spmd.clone, body=%wide.region_5.7_spmd.clone.sunk | while | flops 786563 | bytes 91005 | solution.py:35
  165.6 0.7 compare_select_fusion.10
  166.8 0.7 compare_select_fusion.10
  167.9 0.7 compare_select_fusion.10
  169.1 0.7 compare_select_fusion.10
  170.2 0.7 compare_select_fusion.10
  171.4 0.7 compare_select_fusion.10
  172.6 0.7 compare_select_fusion.10
  173.7 0.7 compare_select_fusion.10
  174.9 0.7 compare_select_fusion.10
  176.0 0.7 compare_select_fusion.10
  177.2 0.7 compare_select_fusion.10
  178.4 0.7 compare_select_fusion.10
  179.5 0.7 compare_select_fusion.10
  180.7 0.7 compare_select_fusion.10
  181.8 0.7 compare_select_fusion.10
  183.0 0.7 compare_select_fusion.10
  184.2 0.7 compare_select_fusion.10
  185.3 0.7 compare_select_fusion.10
  186.5 0.7 compare_select_fusion.10
  187.6 0.7 compare_select_fusion.10
  188.8 0.7 compare_select_fusion.10
  190.0 0.7 compare_select_fusion.10
  191.1 0.7 compare_select_fusion.10
  192.3 0.7 compare_select_fusion.10
  193.4 0.7 compare_select_fusion.10
  194.6 0.7 compare_select_fusion.10
  195.7 0.7 compare_select_fusion.10
  196.9 0.7 compare_select_fusion.10
  198.1 0.7 compare_select_fusion.10
  199.2 0.7 compare_select_fusion.10
  200.4 0.7 compare_select_fusion.10
  201.5 0.7 compare_select_fusion.10
  202.7 0.7 compare_select_fusion.10
  203.9 0.7 compare_select_fusion.10
  205.0 0.7 compare_select_fusion.10
  206.2 0.7 compare_select_fusion.10
  207.3 0.7 compare_select_fusion.10
  208.5 0.7 compare_select_fusion.10
  209.7 0.7 compare_select_fusion.10
  210.8 0.7 compare_select_fusion.10
  211.5 1.3 dynamic-slice
  213.6 23.5 %all-reduce = f32[256]{0:T(256)S(1)} all-reduce(f32[256]{0:T(256)S(1)} %fusion.40), channel_id=1, replica_groups=mesh['row'=16,'col'=32] {'row'}, use_global_device_ids=true, to_apply=%add | all-reduce | flops 256 | bytes 2048
  237.4 10.5 %while.35 = (s32[]{:T(128)}, f32[16,8192]{1,0:T(8,128)S(1)}, s32[16,16]{1,0:T(8,128)S(1)}, s32[8192]{0:T(1024)S(1)}, s32[16,16]{1,0:T(8,128)S(1)}, /*index=5*/f3...) while((s32[]{:T(128)}, f32[16,8192]{1,0:T(8,128)S(1)}, ...), condition=%wide.region_10.11_spmd, body=%wide.region_8.10_spmd.sunk | while | flops 1441810 | bytes 181013 | solution.py:137
  237.4 0.4 fusion.54
  247.9 23.0 %gather_fusion = s32[4096]{0:T(1024)S(1)} fusion(s32[8192]{0:T(1024)S(1)} %get-tuple-element.538, s32[4096]{0:T(1024)S(1)} %get-tuple-element.264), kind=kCustom, calls=%fused_computation | custom fusion | bytes 49152 | tf_op jit(solution)/shard_map/gather | solution.py:75
  270.9 23.0 %gather_fusion.3 = f32[4096]{0:T(1024)S(1)} fusion(f32[8192]{0:T(1024)S(1)} %get-tuple-element.537, s32[4096]{0:T(1024)S(1)} %get-tuple-element.264), kind=kCustom, calls=%fused_computation.3 | custom fusion | bytes 49152 | tf_op jit(solution)/shard_map/gather | solution.py:73
  294.1 140.3 %psum.15 = f32[8192]{0:T(1024)S(1)} all-reduce(f32[8192]{0:T(1024)S(1)} %reduce_sum.48), channel_id=1, replica_groups=mesh['row'=16,'col'=32] {'col'}, use_global_device_ids=true, to_apply=%region_12.13 | all-reduce | flops 8192 | bytes 65536 | tf_op jit(solution)/shard_map/psum | solution.py:138
  434.5 23.0 %gather_fusion.2 = f32[4096]{0:T(1024)S(1)} fusion(f32[8192]{0:T(1024)S(1)} %get-tuple-element.267, s32[4096]{0:T(1024)S(1)} %get-tuple-element.264), kind=kCustom, calls=%fused_computation.2 | custom fusion | bytes 49152 | tf_op jit(solution)/shard_map/gather | solution.py:74
  457.5 8.1 %while.36 = (s32[]{:T(128)}, f32[16,16]{1,0:T(8,128)S(1)}, s32[16,16]{1,0:T(8,128)S(1)}, s32[8192]{0:T(1024)S(1)}, f32[1,8192]{1,0:T(1,128)S(1)}, /*index=5*/f32...) while((s32[]{:T(128)}, f32[16,16]{1,0:T(8,128)S(1)}, ...), condition=%wide.region_15.16_spmd, body=%wide.region_13.15_spmd.sunk | while | flops 925714 | bytes 115569 | solution.py:144
  465.7 19.3 %fusion.34 = f32[512,256]{0,1:T(8,128)S(1)} fusion(f32[512,4096]{1,0:T(8,128)} %all-gather.2.cloned.1.call-done, s32[256]{0:T(256)S(1)} %iota_add_fusion, f32[256]{0:T(256)S(1)} %div.58, f32[256]{0:T(256)S(1)} %all-reduce, f32[256]{0:T(256)S(1)} %dynamic_slice.52, f32[4096]{0:T(1024)S(1)} %gather_fusion.3, f32[4096]{0:T(1024)S(1)} %gather_fusion.2, ...), kind=kOutput, calls=%fused_computation.60 | convolution fusion | flops 6452936704 | bytes 8970496 | tf_op jit(solution)/shard_map/dot_general | solution.py:160
  485.0 1.0 copy.8
  (331 shorter events, 36.7 us)
Async XLA Ops:
  6.5 111.8 %copy-start = (f32[8192]{0:T(1024)S(1)}, f32[8192]{0:T(1024)}, u32[]{:S(2)}) copy-start(f32[8192]{0:T(1024)} %param.12) | copy-start | bytes 98308
  6.5 459.1 %all-gather.2.cloned.1.call-start = ((), (), s32[]{:S(2)}) async-start(), calls=%async_computation | async-start | bytes 8650752 | tf_op jit(solution)/shard_map/all_gather | solution.py:147
  118.3 95.1 %copy-start.1 = (s32[8192]{0:T(1024)S(1)}, s32[8192]{0:T(1024)}, u32[]{:S(2)}) copy-start(s32[8192]{0:T(1024)} %param.13) | copy-start | bytes 98308
  118.3 129.6 %copy-start.2 = (s32[8192]{0:T(1024)S(1)}, s32[8192]{0:T(1024)}, u32[]{:S(2)}) copy-start(s32[8192]{0:T(1024)} %param.14) | copy-start | bytes 98308
Sparse Core Ops, SparseCore 0:
  10.4 114.0 all-gather.1
where the time goes:
time: 494 us; the launch traced here: 493 us
  blocking collectives  236 us (48%)
  local copies, waits for them, and re-layouts  152 us (31%)
  other arithmetic  65.8 us (13%)
  matrix products  19.3 us (4%)
  between operations  15.6 us (3%)
    psum x1, blocking collectives, shards(): log_sum = lax.psum(partial_logs, 'col')  140 us
    all_gather x1, blocking collectives, shards(): edge_rows = lax.all_gather(edge_rows, 'col', axis=1, tiled=True)  49 us
    gather x1, local copies, waits for them, and re-layouts, bracket_lengths(): next_gap = pole_values[jnp.minimum(following, order_size - 1)] - pole_values  45.5 us
    scatter x1, local copies, waits for them, and re-layouts, shards(): spread = jnp.zeros((order_size,), jnp.float32).at[position].set(boundary)  30.5 us
    select_n x40, other arithmetic, halving(): jnp.where(is_below, high_end, middle)  26.3 us
    psum x1, blocking collectives, shards(): edge_rows = lax.psum(edge_rows, 'row')  23.6 us
    unnamed x1, blocking collectives  23.5 us
    gather x1, local copies, waits for them, and re-layouts, cauchy_tile(): row_live = live_mask[sorted_rows] > 0  23 us
  transfers between devices with their start and end apart: 1, of which 0 were waited for; matrix products, arithmetic and copies ran while one was open for 44% of the time, Pallas kernels for 0%

commit v1 on v0

--- a/solution.py
+++ b/solution.py
@@ -105,7 +105,9 @@
         ]
     )
     edge_rows = lax.psum(edge_rows, "row")
-    edge_rows = lax.all_gather(edge_rows, "col", axis=1, tiled=True)
+    edge_rows = jnp.concatenate(
+        lax.all_to_all(jnp.stack([edge_rows] * lax.axis_size("col")), "col", 0, 0), axis=1
+    )
     boundary = jnp.concatenate([edge_rows[0], edge_rows[1]])
     spread = jnp.zeros((order_size,), jnp.float32).at[position].set(boundary)
     coupling = jnp.where(live_mask > 0, spread, 0.0)

time: 494 us -> 461 us (0.933)
  blocking collectives: 236 us -> 190 us
  starting transfers between devices: 0.01 us -> 13.5 us
    all_gather x1 -> x0, blocking collectives: 49 us -> none  [shards(): edge_rows = lax.all_gather(edge_rows, 'col', axis=1, tiled=True)]
    all_to_all x0 -> x1, starting transfers between devices: none -> 13.5 us  [shards(): lax.all_to_all(jnp.stack([edge_rows] * lax.axis_size('col')), 'col', 0, 0)]
  transfers between devices with their start and end apart: 1 -> 2, of which waited for: 0 -> 0; matrix products, arithmetic and copies ran while one was open for 44% -> 47% of each run, Pallas kernels for 0% -> 0%
where the time goes in v1:
time: 461 us; the launch traced here: 460 us
  blocking collectives  190 us (41%)
  local copies, waits for them, and re-layouts  153 us (33%)
  other arithmetic  65.7 us (14%)
  matrix products  19.3 us (4%)
  between operations  15.6 us (3%)
  starting transfers between devices  13.5 us (3%)
    psum x1, blocking collectives, shards(): log_sum = lax.psum(partial_logs, 'col')  143 us
    gather x1, local copies, waits for them, and re-layouts, bracket_lengths(): next_gap = pole_values[jnp.minimum(following, order_size - 1)] - pole_values  45.5 us
    scatter x1, local copies, waits for them, and re-layouts, shards(): spread = jnp.zeros((order_size,), jnp.float32).at[position].set(boundary)  30.5 us
    select_n x40, other arithmetic, halving(): jnp.where(is_below, high_end, middle)  26.3 us
    psum x1, blocking collectives, shards(): edge_rows = lax.psum(edge_rows, 'row')  23.6 us
    unnamed x1, blocking collectives  23.5 us
    gather x1, local copies, waits for them, and re-layouts, cauchy_tile(): row_live = live_mask[sorted_rows] > 0  23 us
    gather x1, local copies, waits for them, and re-layouts, cauchy_tile(): row_poles = pole_values[sorted_rows]  23 us
  transfers between devices with their start and end apart: 2, of which 0 were waited for; matrix products, arithmetic and copies ran while one was open for 47% of the time, Pallas kernels for 0%

profile of v1, /device:TPU:32, one launch (start us, length us, event | category | flops | bytes accessed | tf_op | source)
XLA Modules:
  0.0 460.3 jit_solution(18235172250339332462)
XLA Ops:
  6.5 0.7 all-gather.2.cloned.1.call-update
  7.3 0.7 broadcast_select_fusion.2
  8.0 23.6 %psum.14 = f32[2,128]{1,0:T(2,128)S(1)} all-reduce(f32[2,128]{1,0:T(2,128)S(1)} %pad_maximum_fusion.1), channel_id=1, replica_groups=mesh['row'=16,'col'=32] {'row'}, use_global_device_ids=true, to_apply=%region_0.1 | all-reduce | flops 256 | bytes 2048 | tf_op jit(solution)/shard_map/psum | solution.py:107
  31.5 0.6 stack.5
  32.2 13.5 %all-to-all-start = ((f32[32,2,128]{2,1,0:T(2,128)}), f32[32,2,128]{2,1,0:T(2,128)S(1)}, u32[]{:S(2)}, u32[]{:S(2)}) async-start(f32[32,2,128]{2,1,0:T(2,128)} %stack.5), calls=%async_computation | async-start | bytes 65536 | tf_op jit(solution)/shard_map/all_to_all | solution.py:109
  45.8 0.8 compare_select_fusion.4
  46.5 0.8 broadcast_compare_fusion.4
  47.3 0.8 dynamic_slice.52
  48.1 0.7 fusion.37
  48.8 23.0 %gather_fusion = s32[4096]{0:T(1024)S(1)} fusion(s32[8192]{0:T(1024)S(1)} %copy-done.1, s32[4096]{0:T(1024)S(1)} %get-tuple-element.264), kind=kCustom, calls=%fused_computation | custom fusion | bytes 49152 | tf_op jit(solution)/shard_map/gather | solution.py:75
  71.9 23.0 %gather_fusion.3 = f32[4096]{0:T(1024)S(1)} fusion(f32[8192]{0:T(1024)S(1)} %copy-done, s32[4096]{0:T(1024)S(1)} %get-tuple-element.264), kind=kCustom, calls=%fused_computation.3 | custom fusion | bytes 49152 | tf_op jit(solution)/shard_map/gather | solution.py:73
  95.8 1.2 dynamic-slice
  97.6 30.5 %scatter_custom_fusion = f32[8192]{0:T(1024)S(1)} fusion(s32[8192]{0:T(1024)S(1)} %compare_select_fusion.4, f32[8192]{0:T(1024)S(1)} %pad_maximum_fusion, f32[]{:T(128)} %constant.114.clone.1), kind=kCustom, calls=%fused_computation.74 | custom fusion | bytes 32772 | tf_op jit(solution)/shard_map/scatter | solution.py:112
  128.1 0.6 fusion.44
  128.9 2.3 reduce-window.9
  132.2 45.5 %gather_fusion.1 = f32[8192]{0:T(1024)S(1)} fusion(f32[8192]{0:T(1024)S(1)} %copy-done, s32[8192]{0:T(1024)S(1)} %broadcast_clamp_fusion), kind=kCustom, calls=%fused_computation.1 | custom fusion | bytes 98304 | tf_op jit(solution)/shard_map/gather | solution.py:16
  178.5 46.3 %while.37 = (s32[]{:T(128)}, f32[16]{0:T(128)S(1)}, f32[16]{0:T(128)S(1)}, f32[]{:T(128)}, pred[1,8192]{1,0:T(4,128)(4,1)S(1)}, /*index=5*/f32[8192]{0:T(1024)S(...) while((s32[]{:T(128)}, f32[16]{0:T(128)S(1)}, ...), condition=%wide.region_7.8_spmd.clone, body=%wide.region_5.7_spmd.clone.sunk | while | flops 786563 | bytes 91005 | solution.py:35
  178.9 0.7 compare_select_fusion.10
  180.1 0.7 compare_select_fusion.10
  181.3 0.7 compare_select_fusion.10
  182.4 0.7 compare_select_fusion.10
  183.6 0.7 compare_select_fusion.10
  184.7 0.7 compare_select_fusion.10
  185.9 0.7 compare_select_fusion.10
  187.1 0.7 compare_select_fusion.10
  188.2 0.7 compare_select_fusion.10
  189.4 0.7 compare_select_fusion.10
  190.5 0.7 compare_select_fusion.10
  191.7 0.7 compare_select_fusion.10
  192.8 0.7 compare_select_fusion.10
  194.0 0.7 compare_select_fusion.10
  195.2 0.7 compare_select_fusion.10
  196.3 0.7 compare_select_fusion.10
  197.5 0.7 compare_select_fusion.10
  198.6 0.7 compare_select_fusion.10
  199.8 0.7 compare_select_fusion.10
  201.0 0.7 compare_select_fusion.10
  202.1 0.7 compare_select_fusion.10
  203.3 0.7 compare_select_fusion.10
  204.4 0.7 compare_select_fusion.10
  205.6 0.7 compare_select_fusion.10
  206.8 0.7 compare_select_fusion.10
  207.9 0.7 compare_select_fusion.10
  209.1 0.7 compare_select_fusion.10
  210.2 0.7 compare_select_fusion.10
  211.4 0.7 compare_select_fusion.10
  212.5 0.7 compare_select_fusion.10
  213.7 0.7 compare_select_fusion.10
  214.9 0.7 compare_select_fusion.10
  216.0 0.7 compare_select_fusion.10
  217.2 0.7 compare_select_fusion.10
  218.3 0.7 compare_select_fusion.10
  219.5 0.7 compare_select_fusion.10
  220.7 0.7 compare_select_fusion.10
  221.8 0.7 compare_select_fusion.10
  223.0 0.7 compare_select_fusion.10
  224.1 0.7 compare_select_fusion.10
  225.0 23.5 %all-reduce = f32[256]{0:T(256)S(1)} all-reduce(f32[256]{0:T(256)S(1)} %fusion.40), channel_id=1, replica_groups=mesh['row'=16,'col'=32] {'row'}, use_global_device_ids=true, to_apply=%add | all-reduce | flops 256 | bytes 2048
  248.6 10.4 %while.35 = (s32[]{:T(128)}, f32[16,8192]{1,0:T(8,128)S(1)}, s32[16,16]{1,0:T(8,128)S(1)}, s32[8192]{0:T(1024)S(1)}, s32[16,16]{1,0:T(8,128)S(1)}, /*index=5*/f3...) while((s32[]{:T(128)}, f32[16,8192]{1,0:T(8,128)S(1)}, ...), condition=%wide.region_10.11_spmd, body=%wide.region_8.10_spmd.sunk | while | flops 1441810 | bytes 181013 | solution.py:139
  259.1 142.8 %psum.15 = f32[8192]{0:T(1024)S(1)} all-reduce(f32[8192]{0:T(1024)S(1)} %reduce_sum.48), channel_id=1, replica_groups=mesh['row'=16,'col'=32] {'col'}, use_global_device_ids=true, to_apply=%region_12.13 | all-reduce | flops 8192 | bytes 65536 | tf_op jit(solution)/shard_map/psum | solution.py:140
  401.9 23.0 %gather_fusion.2 = f32[4096]{0:T(1024)S(1)} fusion(f32[8192]{0:T(1024)S(1)} %get-tuple-element.267, s32[4096]{0:T(1024)S(1)} %get-tuple-element.264), kind=kCustom, calls=%fused_computation.2 | custom fusion | bytes 49152 | tf_op jit(solution)/shard_map/gather | solution.py:74
  425.0 8.1 %while.36 = (s32[]{:T(128)}, f32[16,16]{1,0:T(8,128)S(1)}, s32[16,16]{1,0:T(8,128)S(1)}, s32[8192]{0:T(1024)S(1)}, f32[1,8192]{1,0:T(1,128)S(1)}, /*index=5*/f32...) while((s32[]{:T(128)}, f32[16,16]{1,0:T(8,128)S(1)}, ...), condition=%wide.region_15.16_spmd, body=%wide.region_13.15_spmd.sunk | while | flops 925714 | bytes 115569 | solution.py:146
  433.1 19.3 %fusion.34 = f32[512,256]{0,1:T(8,128)S(1)} fusion(f32[512,4096]{1,0:T(8,128)} %all-gather.2.cloned.1.call-done, s32[256]{0:T(256)S(1)} %iota_add_fusion, f32[256]{0:T(256)S(1)} %div.58, f32[256]{0:T(256)S(1)} %all-reduce, f32[256]{0:T(256)S(1)} %dynamic_slice.52, f32[4096]{0:T(1024)S(1)} %gather_fusion.3, f32[4096]{0:T(1024)S(1)} %gather_fusion.2, ...), kind=kOutput, calls=%fused_computation.60 | convolution fusion | flops 6452936704 | bytes 8970496 | tf_op jit(solution)/shard_map/dot_general | solution.py:162
  452.4 1.0 copy.8
  (331 shorter events, 37.6 us)
Async XLA Ops:
  6.5 42.3 %copy-start.1 = (s32[8192]{0:T(1024)S(1)}, s32[8192]{0:T(1024)}, u32[]{:S(2)}) copy-start(s32[8192]{0:T(1024)} %param.13) | copy-start | bytes 98308
  6.5 426.6 %all-gather.2.cloned.1.call-start = ((), (), s32[]{:S(2)}) async-start(), calls=%async_computation.1 | async-start | bytes 8650752 | tf_op jit(solution)/shard_map/all_gather | solution.py:149
  32.2 65.4 %all-to-all-start = ((f32[32,2,128]{2,1,0:T(2,128)}), f32[32,2,128]{2,1,0:T(2,128)S(1)}, u32[]{:S(2)}, u32[]{:S(2)}) async-start(f32[32,2,128]{2,1,0:T(2,128)} %stack.5), calls=%async_computation | async-start | bytes 65536 | tf_op jit(solution)/shard_map/all_to_all | solution.py:109
  48.8 23.1 %copy-start = (f32[8192]{0:T(1024)S(1)}, f32[8192]{0:T(1024)}, u32[]{:S(2)}) copy-start(f32[8192]{0:T(1024)} %param.12) | copy-start | bytes 98308
Sparse Core Ops, SparseCore 0:
  10.4 114.1 all-gather.1
